TPU v7x, 32 devices: a whole 2x2x4 slice. The times are simulated.
32 devices in a mesh: batch: 4 (over z), pos: 8 (over y, x, core).
Axes of the slice: x: 2, y: 2, z: 4, core: 2. Of those that a mesh axis runs over, the one named last changes fastest.
Arguments:
- inputs: bfloat16 [4, 4096, 1536], P('batch', 'pos'), may hold values from -6 to 6
- bn_scale: float32 [1536], replicated, may hold values from 0.25 to 1.75
- bn_shift: float32 [1536], replicated, may hold values from -2 to 2
- mid_scale: float32 [384], replicated, may hold values from 0.25 to 1.75
- mid_shift: float32 [384], replicated, may hold values from -2 to 2
- dilated_weight: bfloat16 [1536, 3, 384], P('batch'), may hold values from -0.09375 to 0.09375
- w_point: bfloat16 [384, 1536], P('batch'), may hold values from -0.3125 to 0.3125
- head: bfloat16 [5120, 1536], P('pos'), may hold values from -0.15625 to 0.15625
- targets: bfloat16 [4, 4096, 512], P('batch', 'pos'), may hold values from 0 to 2
- assay_slots: int32 [4, 512], P('batch', 'pos'), may hold values from 0 to 639, as said below
- assay_counts: int32 [4, 8], P('batch', 'pos'), may hold values from 1 to 64, as said below
Outputs:
- d_inputs: bfloat16 [4, 4096, 1536], P('batch', 'pos')
- new_head: bfloat16 [5120, 1536], P('pos')
Inputs may be any that keep to these rules, and one draw needn't show every extreme that they name: `assay_slots`: within each block of 64 slots (one shard of one sequence) the entries are distinct. `assay_counts`: in every sequence some shard has all 64 slots live.
All inputs are finite; a program needn't handle non-finite values.
Results may differ from a plain program's by a relative error of at most 0.012.
Values may be sent and summed in bfloat16 or wider, within the bound.
A program may use at most 64 MiB of HBM per device.

v0:
```python
import jax
import jax.numpy as jnp
from jax import lax
from jax.sharding import PartitionSpec as P

DILATION_STEP = 32


def with_halo(shard, sides, width):
    for axis, dim in sides:
        peers, length = (lax.axis_size(axis), shard.shape[dim])
        up = [(i, (i + 1) % peers) for i in range(peers - 1)]
        down = [(j, i) for i, j in up]
        last = lax.slice_in_dim(shard, length - width, length, axis=dim)
        initial = lax.slice_in_dim(shard, 0, width, axis=dim)
        before = lax.ppermute(last, axis, up)
        after = lax.ppermute(initial, axis, down)
        shard = jnp.concatenate([before, shard, after], axis=dim)
    return shard


def gelu_slope(value):
    return jax.jvp(jax.nn.gelu, (value,), (jnp.ones_like(value),))[1]


def per_device(
    inputs,
    bn_scale,
    bn_shift,
    mid_scale,
    mid_shift,
    dilated_weight,
    w_point,
    head,
    targets,
    assay_slots,
    assay_counts,
):
    contract = (((1,), (1,)), ((), ()))
    kernel, pointwise = (
        lax.all_gather(dilated_weight, "batch", axis=0, tiled=True),
        lax.all_gather(w_point, "batch", axis=0, tiled=True),
    )
    stream = inputs[0]
    rows = stream.shape[0]
    window_length = DILATION_STEP
    first = stream.astype(jnp.float32) * bn_scale + bn_shift
    acted = jax.nn.gelu(first).astype(jnp.bfloat16)
    padded_input = with_halo(acted, (("pos", 0),), window_length)
    hidden_state = jnp.dot(
        padded_input[0:rows], kernel[:, 0, :], preferred_element_type=jnp.float32
    )
    hidden_state = hidden_state + jnp.dot(
        padded_input[window_length : window_length + rows],
        kernel[:, 1, :],
        preferred_element_type=jnp.float32,
    )
    hidden_state = hidden_state + jnp.dot(
        padded_input[2 * window_length : 2 * window_length + rows],
        kernel[:, 2, :],
        preferred_element_type=jnp.float32,
    )
    second = hidden_state * mid_scale + mid_shift
    mid = jax.nn.gelu(second).astype(jnp.bfloat16)
    embed = (
        stream.astype(jnp.float32) + jnp.dot(mid, pointwise, preferred_element_type=jnp.float32)
    ).astype(jnp.bfloat16)
    slots = assay_slots[0]
    slot_count = slots.shape[0]
    chosen = head[slots]
    live_mark = (jnp.arange(slot_count) < assay_counts[0, 0]).astype(jnp.bfloat16)
    selected, live_all = (
        lax.all_gather(chosen, "pos", axis=0, tiled=True),
        lax.all_gather(live_mark, "pos", axis=0, tiled=True),
    )
    pre = lax.dot_general(embed, selected, contract, preferred_element_type=jnp.float32)
    goal = targets[0].astype(jnp.float32)
    delta = (
        live_all.astype(jnp.float32) * (jax.nn.softplus(pre) - goal) * jax.nn.sigmoid(pre)
    ).astype(jnp.bfloat16)
    back = jnp.dot(delta, selected, preferred_element_type=jnp.float32).astype(jnp.bfloat16)
    dmid = lax.dot_general(back, pointwise, contract, preferred_element_type=jnp.float32)
    dhid = (dmid * gelu_slope(second) * mid_scale).astype(jnp.bfloat16)
    padded_grad = with_halo(dhid, (("pos", 0),), window_length)
    dact = lax.dot_general(
        padded_grad[2 * window_length : 2 * window_length + rows],
        kernel[:, 0, :],
        contract,
        preferred_element_type=jnp.float32,
    )
    dact = dact + lax.dot_general(
        padded_grad[window_length : window_length + rows],
        kernel[:, 1, :],
        contract,
        preferred_element_type=jnp.float32,
    )
    dact = dact + lax.dot_general(
        padded_grad[0:rows], kernel[:, 2, :], contract, preferred_element_type=jnp.float32
    )
    d_inputs = (back.astype(jnp.float32) + dact * gelu_slope(first) * bn_scale).astype(jnp.bfloat16)
    owned = lax.psum_scatter(
        lax.dot_general(
            delta, embed, (((0,), (0,)), ((), ())), preferred_element_type=jnp.float32
        ).astype(jnp.bfloat16),
        "pos",
        scatter_dimension=0,
        tiled=True,
    ).astype(jnp.float32)
    spread = jnp.zeros((head.shape[0], owned.shape[1]), jnp.float32).at[slots].add(owned)
    d_head = lax.psum(spread.astype(jnp.bfloat16), "batch").astype(jnp.float32)
    new_head = (head.astype(jnp.float32) - 0.004 * d_head).astype(jnp.bfloat16)
    return (d_inputs[None], new_head)


def solution(mesh):
    in_specs = (
        P("batch", "pos", None),
        P(),
        P(),
        P(),
        P(),
        P("batch", None, None),
        P("batch", None),
        P("pos", None),
        P("batch", "pos", None),
        P("batch", "pos"),
        P("batch", "pos"),
    )
    out_specs = (P("batch", "pos", None), P("pos", None))
    return jax.shard_map(
        per_device, mesh=mesh, in_specs=in_specs, out_specs=out_specs, check_vma=False
    )
```

profile of v0, /device:TPU:0, one launch (start us, length us, event | category | flops | bytes accessed | tf_op | source)
XLA Modules:
  0.0 286.1 jit_solution(2264082619135657359)
XLA Ops:
  9.4 3.4 %gather_fusion = bf16[64,1536]{1,0:T(8,128)(2,1)} fusion(bf16[640,1536]{1,0:T(8,128)(2,1)} %param.18, s32[1024]{0:T(1024)S(1)} %pad_clamp_fusion), kind=kCustom, calls=%fused_computation | custom fusion | bytes 393472 | tf_op jit(solution)/shard_map/gather | solution.py:70
  12.9 1.3 fusion.12
  14.2 2.4 collective-permute-start
  16.6 1.3 collective-permute-start.1
  19.9 17.5 %all-reduce = bf16[512]{0:T(512)(128)(2,1)S(1)} all-reduce(bf16[512]{0:T(512)(128)(2,1)S(1)} %dynamic-update-slice), channel_id=1, replica_groups=mesh['batch'=4,'pos'=8] {'pos'}, use_global_device_ids=true, to_apply=%add | all-reduce | flops 512 | bytes 2048
  37.4 44.9 %all-gather.5.cloned.1.call-done = bf16[1536,3,384]{2,0,1:T(8,128)(2,1)} async-done(((bf16[384,3,384]{2,0,1:T(8,128)(2,1)}), bf16[1536,3,384]{2,0,1:T(8,128)(2,1)}) %all-gather.5.cloned.1.call-update) | async-done | bytes 3538960 | tf_op jit(solution)/shard_map/all_gather | solution.py:41
  82.3 2.8 fusion.38
  85.2 1.9 fusion.34
  87.1 1.9 fusion.44
  89.0 23.9 %all-gather.7.cloned.1.call-done = bf16[384,1536]{1,0:T(8,128)(2,1)} async-done(((bf16[96,1536]{1,0:T(8,128)(2,1)}), bf16[384,1536]{1,0:T(8,128)(2,1)}) %all-gather.7.cloned.1.call-update) | async-done | bytes 1179664 | tf_op jit(solution)/shard_map/all_gather | solution.py:42
  113.0 2.5 fusion.29
  115.5 24.8 %all-gather.9.cloned.1.call-done = bf16[512,1536]{1,0:T(8,128)(2,1)} async-done(((bf16[64,1536]{1,0:T(8,128)(2,1)}), bf16[512,1536]{1,0:T(8,128)(2,1)}) %all-gather.9.cloned.1.call-update) | async-done | bytes 1572880 | tf_op jit(solution)/shard_map/all_gather | solution.py:73
  140.3 2.5 fusion.90
  143.7 4.3 %convolution_convert_fusion = bf16[512,1536]{1,0:T(8,128)(2,1)} fusion(bf16[512,1536]{1,0:T(8,128)(2,1)} %copy-done.12, f32[512,512]{1,0:T(8,128)S(1)} %fusion.90, bf16[1,512,512]{2,1,0:T(8,128)(2,1)S(1)} %copy-done.8, f32[512]{0:T(512)S(1)} %convert_element_type.70), kind=kOutput, calls=%fused_computation.39 | convolution fusion | flops 809762816 | bytes 4720640 | tf_op jit(solution)/shard_map/dot_general | solution.py:102
  148.2 4.1 %convolution_convert_fusion.1 = bf16[512,1536]{1,0:T(8,128)(2,1)} fusion(bf16[512,1536]{1,0:T(8,128)(2,1)S(1)} %copy-done.6, f32[512,512]{1,0:T(8,128)} %copy-done.13, bf16[1,512,512]{2,1,0:T(8,128)(2,1)} %param.19, f32[512]{0:T(512)S(1)} %convert_element_type.70), kind=kOutput, calls=%fused_computation.40 | convolution fusion | flops 809762816 | bytes 4720640 | tf_op jit(solution)/shard_map/dot_general | solution.py:81
  152.2 34.5 %reduce-scatter.2.cloned.1.call-done = bf16[64,1536]{1,0:T(8,128)(2,1)} async-done(((bf16[512,1536]{1,0:T(8,128)(2,1)}), bf16[64,1536]{1,0:T(8,128)(2,1)}) %reduce-scatter.2.cloned.1.call-update) | async-done | bytes 196624 | tf_op jit(solution)/shard_map/reduce_scatter | solution.py:101
  186.7 3.7 %scatter_custom_fusion = f32[640,1536]{1,0:T(8,128)} fusion(s32[64]{0:T(128)S(1)} %fusion.71, f32[]{:T(128)} %constant.15.clone.1, bf16[64,1536]{1,0:T(8,128)(2,1)} %reduce-scatter.2.cloned.1.call-done), kind=kCustom, calls=%fused_computation.43 | custom fusion | flops 196608 | bytes 4128772 | tf_op jit(solution)/shard_map/scatter-add | solution.py:109
  190.4 3.7 %convert_element_type.89 = bf16[640,1536]{1,0:T(8,128)(2,1)} convert(f32[640,1536]{1,0:T(8,128)} %scatter_custom_fusion) | non-fusion elementwise | flops 983040 | bytes 5898240 | tf_op jit(solution)/shard_map/convert_element_type | solution.py:110
  194.1 3.0 %fusion.45 = bf16[512,384]{1,0:T(8,128)(2,1)S(1)} fusion(bf16[512,1536]{1,0:T(8,128)(2,1)} %convolution_convert_fusion.1, bf16[384,1536]{1,0:T(8,128)(2,1)S(1)} %copy-done.7, f32[512,384]{1,0:T(8,128)} %fusion.44, f32[384]{0:T(512)S(1)} %copy-done.10), kind=kOutput, calls=%fused_computation.59 | convolution fusion | flops 607715328 | bytes 3933696 | tf_op jit(solution)/shard_map/dot_general | solution.py:82
  197.2 1.3 collective-permute-start.2
  198.5 3.0 %collective-permute-start.3 = (bf16[32,384]{1,0:T(8,128)(2,1)S(1)}, bf16[32,384]{1,0:T(8,128)(2,1)S(1)}, u32[]{:S(2)}, u32[]{:S(2)}) collective-permute-start(bf16[32,384]{1,0:T(8,128)(2,1)S(1)} %get-tuple-element.5), channel_id=1, source_target_pairs={{0,1},{1,2},{2,3},{3,4},{4,5},{5,6},{6,7},{8,9},{9,10},{10,11},{11... | collective-permute-start | bytes 73736 | tf_op jit(solution)/shard_map/ppermute | solution.py:16
  204.0 4.0 %fusion.30 = bf16[1,512,1536]{2,1,0:T(8,128)(2,1)} fusion(bf16[1,512,1536]{2,1,0:T(8,128)(2,1)S(1)} %copy-done.1, f32[512,1536]{1,0:T(8,128)S(1)} %fusion.51, f32[512,1536]{1,0:T(8,128)S(1)} %fusion.50, bf16[512,1536]{1,0:T(8,128)(2,1)S(1)} %copy-done.14, f32[1536]{0:T(1024)S(1)} %copy-done.4, f32[1536]{0:T(1024)S(1)} %copy-done.5, ...), kind=kOutput, calls=%fused_computation.42 | convolution fusion | flops 625213440 | bytes 12623872 | tf_op jit(solution)/shard_map/dot_general | solution.py:85
  207.9 68.3 %all-reduce.3.cloned.1.call-done = bf16[640,1536]{1,0:T(8,128)(2,1)} async-done(((bf16[640,1536]{1,0:T(8,128)(2,1)}), bf16[640,1536]{1,0:T(8,128)(2,1)}) %all-reduce.3.cloned.1.call-update) | async-done | bytes 1966096 | tf_op jit(solution)/shard_map/psum | solution.py:110
  276.2 3.4 %subtract_convert_fusion = bf16[640,1536]{1,0:T(8,128)(2,1)} fusion(bf16[640,1536]{1,0:T(8,128)(2,1)} %all-reduce.3.cloned.1.call-done, bf16[640,1536]{1,0:T(8,128)(2,1)S(1)} %copy-done), kind=kLoop, calls=%fused_computation.9 | loop fusion | flops 4915200 | bytes 5898240 | tf_op jit(solution)/shard_map/convert_element_type | solution.py:111
  (55 shorter events, 6.6 us)
Async XLA Ops:
  7.2 11.4 %copy-start.11 = (u32[32]{0:T(128)S(1)}, u32[32]{0:T(128)}, u32[]{:S(2)}) copy-start(u32[32]{0:T(128)} %constant.34) | copy-start | bytes 388
  7.2 5.7 %copy-start.1 = (bf16[1,512,1536]{2,1,0:T(8,128)(2,1)S(1)}, bf16[1,512,1536]{2,1,0:T(8,128)(2,1)}, u32[]{:S(2)}) copy-start(bf16[1,512,1536]{2,1,0:T(8,128)(2,1)} %param.11) | copy-start | bytes 4718596
  7.2 5.7 %copy-start.4 = (f32[1536]{0:T(1024)S(1)}, f32[1536]{0:T(1024)}, u32[]{:S(2)}) copy-start(f32[1536]{0:T(1024)} %param.13) | copy-start | bytes 18436
  7.2 5.7 %copy-start.5 = (f32[1536]{0:T(1024)S(1)}, f32[1536]{0:T(1024)}, u32[]{:S(2)}) copy-start(f32[1536]{0:T(1024)} %param.12) | copy-start | bytes 18436
  7.2 75.1 %all-gather.5.cloned.1.call-start = ((), (), s32[]{:S(2)}) async-start(), calls=%async_computation.1 | async-start | bytes 4423680 | tf_op jit(solution)/shard_map/all_gather | solution.py:41
  7.9 105.0 %all-gather.7.cloned.1.call-start = ((), (), s32[]{:S(2)}) async-start(), calls=%async_computation.2 | async-start | bytes 1474560 | tf_op jit(solution)/shard_map/all_gather | solution.py:42
  8.7 131.6 %all-gather.9.cloned.1.call-start = ((), (), s32[]{:S(2)}) async-start(), calls=%async_computation.5 | async-start | bytes 1769472 | tf_op jit(solution)/shard_map/all_gather | solution.py:73
  12.8 173.9 %reduce-scatter.2.cloned.1.call-start = ((), (), s32[]{:S(2)}) async-start(), calls=%async_computation.3 | async-start | bytes 1769472 | tf_op jit(solution)/shard_map/reduce_scatter | solution.py:101
  14.2 72.9 %collective-permute-start = (bf16[32,1536]{1,0:T(8,128)(2,1)S(1)}, bf16[32,1536]{1,0:T(8,128)(2,1)S(1)}, u32[]{:S(2)}, u32[]{:S(2)}) collective-permute-start(bf16[32,1536]{1,0:T(8,128)(2,1)S(1)} %get-tuple-element.2), channel_id=1, source_target_pairs={{0,1},{1,2},{2,3},{3,4},{4,5},{5,6},{6,7},{8,9},{9,10},{10,11},{11... | collective-permute-start | bytes 294920 | tf_op jit(solution)/shard_map/ppermute | solution.py:16
  16.6 68.6 %collective-permute-start.1 = (bf16[32,1536]{1,0:T(8,128)(2,1)S(1)}, bf16[32,1536]{1,0:T(8,128)(2,1)}, u32[]{:S(2)}, u32[]{:S(2)}) collective-permute-start(bf16[32,1536]{1,0:T(8,128)(2,1)S(1)} %get-tuple-element.3), channel_id=1, source_target_pairs={{1,0},{2,1},{3,2},{4,3},{5,4},{6,5},{7,6},{9,8},{10,9},{11,10},{12... | collective-permute-start | bytes 294920 | tf_op jit(solution)/shard_map/ppermute | solution.py:17
  82.3 2.9 %copy-start.2 = (bf16[1536,3,384]{2,0,1:T(8,128)(2,1)S(1)}, bf16[1536,3,384]{2,0,1:T(8,128)(2,1)}, u32[]{:S(2)}) copy-start(bf16[1536,3,384]{2,0,1:T(8,128)(2,1)} %all-gather.5.cloned.1.call-done) | copy-start | bytes 10616836
  85.1 1.9 copy-start.9
  85.2 1.9 copy-start.10
  115.5 24.8 %copy-start.12 = (bf16[512,1536]{1,0:T(8,128)(2,1)}, bf16[512,1536]{1,0:T(8,128)(2,1)S(1)}, u32[]{:S(2)}) copy-start(bf16[512,1536]{1,0:T(8,128)(2,1)S(1)} %fusion.29) | copy-start | bytes 4718596
  140.3 3.5 %copy-start.8 = (bf16[1,512,512]{2,1,0:T(8,128)(2,1)S(1)}, bf16[1,512,512]{2,1,0:T(8,128)(2,1)}, u32[]{:S(2)}) copy-start(bf16[1,512,512]{2,1,0:T(8,128)(2,1)} %param.19) | copy-start | bytes 1572868
  142.8 1.0 copy-start.13
  143.7 4.4 %copy-start.6 = (bf16[512,1536]{1,0:T(8,128)(2,1)S(1)}, bf16[512,1536]{1,0:T(8,128)(2,1)}, u32[]{:S(2)}) copy-start(bf16[512,1536]{1,0:T(8,128)(2,1)} %all-gather.9.cloned.1.call-done) | copy-start | bytes 4718596
  148.1 128.1 %all-reduce.3.cloned.1.call-start = ((), (), s32[]{:S(2)}) async-start(), calls=%async_computation.4 | async-start | bytes 3932160 | tf_op jit(solution)/shard_map/psum | solution.py:110
  190.4 3.7 %copy-start.7 = (bf16[384,1536]{1,0:T(8,128)(2,1)S(1)}, bf16[384,1536]{1,0:T(8,128)(2,1)}, u32[]{:S(2)}) copy-start(bf16[384,1536]{1,0:T(8,128)(2,1)} %all-gather.7.cloned.1.call-done) | copy-start | bytes 3538948
  194.1 7.4 %copy-start.3 = (bf16[1536,3,384]{2,0,1:T(8,128)(2,1)S(1)}, bf16[1536,3,384]{2,0,1:T(8,128)(2,1)}, u32[]{:S(2)}) copy-start(bf16[1536,3,384]{2,0,1:T(8,128)(2,1)} %all-gather.5.cloned.1.call-done) | copy-start | bytes 10616836
  197.2 6.4 %collective-permute-start.2 = (bf16[32,384]{1,0:T(8,128)(2,1)S(1)}, bf16[32,384]{1,0:T(8,128)(2,1)S(1)}, u32[]{:S(2)}, u32[]{:S(2)}) collective-permute-start(bf16[32,384]{1,0:T(8,128)(2,1)S(1)} %get-tuple-element.4), channel_id=1, source_target_pairs={{1,0},{2,1},{3,2},{4,3},{5,4},{6,5},{7,6},{9,8},{10,9},{11,10},{12... | collective-permute-start | bytes 73736 | tf_op jit(solution)/shard_map/ppermute | solution.py:17
  198.5 4.1 %collective-permute-start.3 = (bf16[32,384]{1,0:T(8,128)(2,1)S(1)}, bf16[32,384]{1,0:T(8,128)(2,1)S(1)}, u32[]{:S(2)}, u32[]{:S(2)}) collective-permute-start(bf16[32,384]{1,0:T(8,128)(2,1)S(1)} %get-tuple-element.5), channel_id=1, source_target_pairs={{0,1},{1,2},{2,3},{3,4},{4,5},{5,6},{6,7},{8,9},{9,10},{10,11},{11... | collective-permute-start | bytes 73736 | tf_op jit(solution)/shard_map/ppermute | solution.py:16
  202.5 1.4 copy-start.14
  203.6 72.6 %copy-start = (bf16[640,1536]{1,0:T(8,128)(2,1)S(1)}, bf16[640,1536]{1,0:T(8,128)(2,1)}, u32[]{:S(2)}) copy-start(bf16[640,1536]{1,0:T(8,128)(2,1)} %param.18) | copy-start | bytes 5898244
Sparse Core Ops, SparseCore 0:
  9.6 72.6 all-gather.4
  83.9 29.0 all-gather.6
  115.4 24.7 all-gather.8
  148.2 38.4 reduce-scatter.1
  194.2 81.9 all-reduce.2
where the time goes:
time: 287 us; the launch traced here: 286 us
  waiting for transfers between devices  198 us (69%)
  matrix products  29 us (10%)
  blocking collectives  17.5 us (6%)
  between operations  15.3 us (5%)
  other arithmetic  12.7 us (4%)
  starting transfers between devices  8.18 us (3%)
  local copies, waits for them, and re-layouts  5.62 us (2%)
    psum x1, waiting for transfers between devices, per_device(): d_head = lax.psum(spread.astype(jnp.bfloat16), 'batch').astype(jnp.float32)  68.3 us
    all_gather x1, waiting for transfers between devices, per_device(): lax.all_gather(dilated_weight, 'batch', axis=0, tiled=True)  44.9 us
    reduce_scatter x1, waiting for transfers between devices, per_device(): lax.psum_scatter(lax.dot_general(delta, embed, (((0,), (0,)), ((), ())),...  34.5 us
    all_gather x1, waiting for transfers between devices, per_device(): lax.all_gather(chosen, 'pos', axis=0, tiled=True)  24.8 us
    all_gather x1, waiting for transfers between devices, per_device(): lax.all_gather(w_point, 'batch', axis=0, tiled=True)  23.9 us
    unnamed x1, blocking collectives  17.5 us
  transfers between devices with their start and end apart: 9, of which 5 were waited for; matrix products, arithmetic and copies ran while one was open for 10% of the time, Pallas kernels for 0%

commit v1 on v0

--- a/solution.py
+++ b/solution.py
@@ -36,6 +36,20 @@
     assay_slots,
     assay_counts,
 ):
+
+    def bring_point_on_mesh(arr):
+        item_now = lax.axis_size("pos")
+        u_next, z, row_out = (item_now, lax.axis_index("pos"), arr.shape[0])
+        f_now, h_now = (arr, 1)
+        while h_now < u_next:
+            base_arr = lax.ppermute(
+                f_now, axis_name="pos", perm=[(kk, (kk - h_now) % u_next) for kk in range(u_next)]
+            )
+            f_now = jnp.concatenate([f_now, base_arr], axis=0)
+            h_now = 2 * h_now
+        front = jnp.roll(f_now, z * row_out, axis=0)
+        return front
+
     contract = (((1,), (1,)), ((), ()))
     kernel, pointwise = (
         lax.all_gather(dilated_weight, "batch", axis=0, tiled=True),
@@ -70,7 +84,7 @@
     chosen = head[slots]
     live_mark = (jnp.arange(slot_count) < assay_counts[0, 0]).astype(jnp.bfloat16)
     selected, live_all = (
-        lax.all_gather(chosen, "pos", axis=0, tiled=True),
+        bring_point_on_mesh(chosen),
         lax.all_gather(live_mark, "pos", axis=0, tiled=True),
     )
     pre = lax.dot_general(embed, selected, contract, preferred_element_type=jnp.float32)

time: 287 us -> 258 us (0.90)
  waiting for transfers between devices: 198 us -> 160 us
  starting transfers between devices: 8.18 us -> 14.1 us
  local copies, waits for them, and re-layouts: 5.62 us -> 11 us
    all_gather x1 -> x0, waiting for transfers between devices: 24.8 us -> none  [per_device(): lax.all_gather(chosen, 'pos', axis=0, tiled=True)]
    all_gather x1, waiting for transfers between devices: 44.9 us -> 27.4 us  [per_device(): lax.all_gather(dilated_weight, 'batch', axis=0, tiled=True)]
    unnamed x33 -> x40, local copies, waits for them, and re-layouts: 2.22 us -> 6.72 us
    ppermute x0 -> x3, starting transfers between devices: none -> 4.11 us  [bring_point_on_mesh(): lax.ppermute(f_now, axis_name='pos', perm=[(kk, (kk - h_now) % u_next) fo...]
    ppermute x0 -> x3, waiting for transfers between devices: none -> 4.03 us  [bring_point_on_mesh(): lax.ppermute(f_now, axis_name='pos', perm=[(kk, (kk - h_now) % u_next) fo...]
  transfers between devices with their start and end apart: 9 -> 11, of which waited for: 5 -> 8; matrix products, arithmetic and copies ran while one was open for 10% -> 13% of each run, Pallas kernels for 0% -> 0%
where the time goes in v1:
time: 258 us
  waiting for transfers between devices  160 us (62%)
  matrix products  27.6 us (11%)
  blocking collectives  15.3 us (6%)
  between operations  15.3 us (6%)
  other arithmetic  15 us (6%)
  starting transfers between devices  14.1 us (5%)
  local copies, waits for them, and re-layouts  11 us (4%)
    psum x1, waiting for transfers between devices, per_device(): d_head = lax.psum(spread.astype(jnp.bfloat16), 'batch').astype(jnp.float32)  69 us
    reduce_scatter x1, waiting for transfers between devices, per_device(): lax.psum_scatter(lax.dot_general(delta, embed, (((0,), (0,)), ((), ())),...  34.1 us
    all_gather x1, waiting for transfers between devices, per_device(): lax.all_gather(dilated_weight, 'batch', axis=0, tiled=True)  27.4 us
    all_gather x1, waiting for transfers between devices, per_device(): lax.all_gather(w_point, 'batch', axis=0, tiled=True)  23.3 us
    unnamed x1, blocking collectives  15.3 us
    ppermute x2, starting transfers between devices, with_halo(): before = lax.ppermute(last, axis, up)  7.27 us
    unnamed x40, local copies, waits for them, and re-layouts  6.72 us
  transfers between devices with their start and end apart: 11, of which 8 were waited for; matrix products, arithmetic and copies ran while one was open for 13% of the time, Pallas kernels for 0%

profile of v1, /device:TPU:0, one launch (start us, length us, event | category | flops | bytes accessed | tf_op | source)
XLA Modules:
  0.0 258.0 jit_solution(12469247922089281049)
XLA Ops:
  9.2 2.7 %gather_fusion = bf16[64,1536]{1,0:T(8,128)(2,1)S(1)} fusion(bf16[640,1536]{1,0:T(8,128)(2,1)} %param.18, s32[1024]{0:T(1024)S(1)} %pad_clamp_fusion), kind=kCustom, calls=%fused_computation | custom fusion | bytes 393472 | tf_op jit(solution)/shard_map/gather | solution.py:84
  11.9 3.4 %collective-permute-start.2 = (bf16[64,1536]{1,0:T(8,128)(2,1)S(1)}, bf16[64,1536]{1,0:T(8,128)(2,1)S(1)}, u32[]{:S(2)}, u32[]{:S(2)}) collective-permute-start(bf16[64,1536]{1,0:T(8,128)(2,1)S(1)} %gather_fusion), channel_id=1, source_target_pairs={{0,7},{1,0},{2,1},{3,2},{4,3},{5,4},{6,5},{7,6},{8,15},{9,8},{10,9... | collective-permute-start | bytes 589832 | tf_op jit(solution)/shard_map/ppermute | solution.py:45
  15.3 2.0 fusion.11
  19.8 1.3 collective-permute-start.1
  21.1 5.5 %collective-permute-start = (bf16[32,1536]{1,0:T(8,128)(2,1)}, bf16[32,1536]{1,0:T(8,128)(2,1)}, u32[]{:S(2)}, u32[]{:S(2)}) collective-permute-start(bf16[32,1536]{1,0:T(8,128)(2,1)} %get-tuple-element.2), channel_id=1, source_target_pairs={{0,1},{1,2},{2,3},{3,4},{4,5},{5,6},{6,7},{8,9},{9,10},{10,11},{11... | collective-permute-start | bytes 294920 | tf_op jit(solution)/shard_map/ppermute | solution.py:16
  28.6 1.9 collective-permute-done.3
  31.7 15.3 %all-reduce = bf16[512]{0:T(512)(128)(2,1)S(1)} all-reduce(bf16[512]{0:T(512)(128)(2,1)S(1)} %dynamic-update-slice), channel_id=1, replica_groups=mesh['batch'=4,'pos'=8] {'pos'}, use_global_device_ids=true, to_apply=%add | all-reduce | flops 512 | bytes 2048
  54.9 27.4 %all-gather.3.cloned.1.call-done = bf16[1536,3,384]{2,0,1:T(8,128)(2,1)} async-done(((bf16[384,3,384]{2,0,1:T(8,128)(2,1)}), bf16[1536,3,384]{2,0,1:T(8,128)(2,1)}) %all-gather.3.cloned.1.call-update) | async-done | bytes 3538960 | tf_op jit(solution)/shard_map/all_gather | solution.py:55
  82.3 3.3 %fusion.36 = f32[512,384]{1,0:T(8,128)S(1)} fusion(bf16[1,512,1536]{2,1,0:T(8,128)(2,1)} %param.11, f32[1536]{0:T(1024)S(1)} %copy-done.5, f32[1536]{0:T(1024)S(1)} %copy-done.6, bf16[1536,3,384]{2,0,1:T(8,128)(2,1)} %all-gather.3.cloned.1.call-done), kind=kOutput, calls=%fused_computation.51 | convolution fusion | flops 613416960 | bytes 3551232 | tf_op jit(solution)/shard_map/dot_general | solution.py:67
  86.7 2.9 %fusion.45 = f32[512,384]{1,0:T(8,128)} fusion(f32[512,384]{1,0:T(8,128)S(1)} %fusion.32, f32[512,384]{1,0:T(8,128)S(1)} %fusion.36, bf16[512,1536]{1,0:T(8,128)(2,1)S(1)} %fusion.11, bf16[32,1536]{1,0:T(8,128)(2,1)} %collective-permute-done, bf16[1536,3,384]{2,0,1:T(8,128)(2,1)S(1)} %copy-done.3, f32[384]{0:T(512)S(1)} %copy-done.11, f32[384]{0:T(512)S(1)} %copy-done.12), kind=kOutput, calls=%fused_computation.60 | convolution fusion | flops 607911936 | bytes 5214208 | tf_op jit(solution)/shard_map/dot_general | solution.py:64
  89.6 23.3 %all-gather.5.cloned.1.call-done = bf16[384,1536]{1,0:T(8,128)(2,1)} async-done(((bf16[96,1536]{1,0:T(8,128)(2,1)}), bf16[384,1536]{1,0:T(8,128)(2,1)}) %all-gather.5.cloned.1.call-update) | async-done | bytes 1179664 | tf_op jit(solution)/shard_map/all_gather | solution.py:56
  112.9 2.5 fusion.27
  115.5 3.1 %fusion.50 = bf16[512,512]{1,0:T(8,128)(2,1)S(1)} fusion(bf16[512,1536]{1,0:T(8,128)(2,1)S(1)} %fusion.27, bf16[1024,1536]{1,0:T(8,128)(2,1)} %constant_dynamic-update-slice_fusion, s32[]{:T(128)S(6)} %select_n.30, bf16[1,512,512]{2,1,0:T(8,128)(2,1)S(1)} %copy-done.10, f32[512]{0:T(512)S(1)} %copy-done.7), kind=kOutput, calls=%fused_computation.70 | convolution fusion | flops 808976384 | bytes 4196356 | tf_op jit(solution)/shard_map/dot_general | solution.py:90
  118.6 2.1 convolution_convert_fusion
  120.8 3.5 %convolution_convert_fusion.1 = bf16[512,1536]{1,0:T(8,128)(2,1)} fusion(bf16[512,512]{1,0:T(8,128)(2,1)S(1)} %fusion.50, bf16[1024,1536]{1,0:T(8,128)(2,1)} %constant_dynamic-update-slice_fusion, s32[]{:T(128)S(6)} %select_n.30), kind=kOutput, calls=%fused_computation.39 | convolution fusion | flops 806092800 | bytes 3670020 | tf_op jit(solution)/shard_map/dot_general | solution.py:95
  124.4 34.1 %reduce-scatter.2.cloned.1.call-done = bf16[64,1536]{1,0:T(8,128)(2,1)} async-done(((bf16[512,1536]{1,0:T(8,128)(2,1)}), bf16[64,1536]{1,0:T(8,128)(2,1)}) %reduce-scatter.2.cloned.1.call-update) | async-done | bytes 196624 | tf_op jit(solution)/shard_map/reduce_scatter | solution.py:115
  158.5 3.7 %scatter_custom_fusion = f32[640,1536]{1,0:T(8,128)} fusion(s32[64]{0:T(128)} %copy-done.8, f32[]{:T(128)} %constant.52.clone.1, bf16[64,1536]{1,0:T(8,128)(2,1)} %reduce-scatter.2.cloned.1.call-done), kind=kCustom, calls=%fused_computation.42 | custom fusion | flops 196608 | bytes 4129280 | tf_op jit(solution)/shard_map/scatter-add | solution.py:123
  162.2 3.7 %convert_element_type.89 = bf16[640,1536]{1,0:T(8,128)(2,1)} convert(f32[640,1536]{1,0:T(8,128)} %scatter_custom_fusion) | non-fusion elementwise | flops 983040 | bytes 5898240 | tf_op jit(solution)/shard_map/convert_element_type | solution.py:124
  166.0 3.0 %fusion.46 = bf16[512,384]{1,0:T(8,128)(2,1)S(1)} fusion(bf16[512,1536]{1,0:T(8,128)(2,1)} %convolution_convert_fusion.1, bf16[384,1536]{1,0:T(8,128)(2,1)S(1)} %copy-done.9, f32[512,384]{1,0:T(8,128)} %fusion.45, f32[384]{0:T(512)S(1)} %copy-done.12), kind=kOutput, calls=%fused_computation.61 | convolution fusion | flops 607715328 | bytes 3933696 | tf_op jit(solution)/shard_map/dot_general | solution.py:96
  169.0 1.7 collective-permute-start.6
  170.7 1.3 collective-permute-start.5
  175.1 4.0 %fusion.28 = bf16[1,512,1536]{2,1,0:T(8,128)(2,1)} fusion(bf16[1,512,1536]{2,1,0:T(8,128)(2,1)S(1)} %copy-done.2, f32[512,1536]{1,0:T(8,128)S(1)} %fusion.52, f32[512,1536]{1,0:T(8,128)S(1)} %fusion.51, bf16[512,1536]{1,0:T(8,128)(2,1)S(1)} %copy-done.14, f32[1536]{0:T(1024)S(1)} %copy-done.5, f32[1536]{0:T(1024)S(1)} %copy-done.6, ...), kind=kOutput, calls=%fused_computation.41 | convolution fusion | flops 625213440 | bytes 12623872 | tf_op jit(solution)/shard_map/dot_general | solution.py:99
  179.0 69.0 %all-reduce.3.cloned.1.call-done = bf16[640,1536]{1,0:T(8,128)(2,1)} async-done(((bf16[640,1536]{1,0:T(8,128)(2,1)}), bf16[640,1536]{1,0:T(8,128)(2,1)}) %all-reduce.3.cloned.1.call-update) | async-done | bytes 1966096 | tf_op jit(solution)/shard_map/psum | solution.py:124
  248.0 3.4 %subtract_convert_fusion = bf16[640,1536]{1,0:T(8,128)(2,1)} fusion(bf16[640,1536]{1,0:T(8,128)(2,1)} %all-reduce.3.cloned.1.call-done, bf16[640,1536]{1,0:T(8,128)(2,1)S(1)} %copy-done), kind=kLoop, calls=%fused_computation.9 | loop fusion | flops 4915200 | bytes 5898240 | tf_op jit(solution)/shard_map/convert_element_type | solution.py:125
  (68 shorter events, 18.3 us)
Async XLA Ops:
  7.2 8.1 %copy-start.1 = (bf16[1,512,1536]{2,1,0:T(8,128)(2,1)S(1)}, bf16[1,512,1536]{2,1,0:T(8,128)(2,1)}, u32[]{:S(2)}) copy-start(bf16[1,512,1536]{2,1,0:T(8,128)(2,1)} %param.11) | copy-start | bytes 4718596
  7.2 75.1 %all-gather.3.cloned.1.call-start = ((), (), s32[]{:S(2)}) async-start(), calls=%async_computation.1 | async-start | bytes 4423680 | tf_op jit(solution)/shard_map/all_gather | solution.py:55
  7.9 105.0 %all-gather.5.cloned.1.call-start = ((), (), s32[]{:S(2)}) async-start(), calls=%async_computation.2 | async-start | bytes 1474560 | tf_op jit(solution)/shard_map/all_gather | solution.py:56
  9.2 18.2 %copy-start.13 = (u32[32]{0:T(128)S(1)}, u32[32]{0:T(128)}, u32[]{:S(2)}) copy-start(u32[32]{0:T(128)} %constant.61) | copy-start | bytes 388
  11.9 6.6 %collective-permute-start.2 = (bf16[64,1536]{1,0:T(8,128)(2,1)S(1)}, bf16[64,1536]{1,0:T(8,128)(2,1)S(1)}, u32[]{:S(2)}, u32[]{:S(2)}) collective-permute-start(bf16[64,1536]{1,0:T(8,128)(2,1)S(1)} %gather_fusion), channel_id=1, source_target_pairs={{0,7},{1,0},{2,1},{3,2},{4,3},{5,4},{6,5},{7,6},{8,15},{9,8},{10,9... | collective-permute-start | bytes 589832 | tf_op jit(solution)/shard_map/ppermute | solution.py:45
  18.5 12.0 %collective-permute-start.3 = (bf16[128,1536]{1,0:T(8,128)(2,1)S(1)}, bf16[128,1536]{1,0:T(8,128)(2,1)S(1)}, u32[]{:S(2)}, u32[]{:S(2)}) collective-permute-start(bf16[128,1536]{1,0:T(8,128)(2,1)S(1)} %pad_maximum_fusion.17), channel_id=1, source_target_pairs={{0,6},{1,7},{2,0},{3,1},{4,2},{5,3},{6,4},{7,5},{8,14},{9,15},{10,... | collective-permute-start | bytes 1179656 | tf_op jit(solution)/shard_map/ppermute | solution.py:45
  19.8 65.8 %collective-permute-start.1 = (bf16[32,1536]{1,0:T(8,128)(2,1)S(1)}, bf16[32,1536]{1,0:T(8,128)(2,1)S(1)}, u32[]{:S(2)}, u32[]{:S(2)}) collective-permute-start(bf16[32,1536]{1,0:T(8,128)(2,1)S(1)} %get-tuple-element.3), channel_id=1, source_target_pairs={{1,0},{2,1},{3,2},{4,3},{5,4},{6,5},{7,6},{9,8},{10,9},{11,10},{12... | collective-permute-start | bytes 294920 | tf_op jit(solution)/shard_map/ppermute | solution.py:17
  21.1 65.6 %collective-permute-start = (bf16[32,1536]{1,0:T(8,128)(2,1)}, bf16[32,1536]{1,0:T(8,128)(2,1)}, u32[]{:S(2)}, u32[]{:S(2)}) collective-permute-start(bf16[32,1536]{1,0:T(8,128)(2,1)} %get-tuple-element.2), channel_id=1, source_target_pairs={{0,1},{1,2},{2,3},{3,4},{4,5},{5,6},{6,7},{8,9},{9,10},{10,11},{11... | collective-permute-start | bytes 294920 | tf_op jit(solution)/shard_map/ppermute | solution.py:16
  26.6 131.9 %reduce-scatter.2.cloned.1.call-start = ((), (), s32[]{:S(2)}) async-start(), calls=%async_computation.3 | async-start | bytes 1769472 | tf_op jit(solution)/shard_map/reduce_scatter | solution.py:115
  31.4 19.4 %collective-permute-start.4 = (bf16[256,1536]{1,0:T(8,128)(2,1)}, bf16[256,1536]{1,0:T(8,128)(2,1)S(1)}, u32[]{:S(2)}, u32[]{:S(2)}) collective-permute-start(bf16[256,1536]{1,0:T(8,128)(2,1)} %pad_maximum_fusion.12), channel_id=1, source_target_pairs={{0,4},{1,5},{2,6},{3,7},{4,0},{5,1},{6,2},{7,3},{8,12},{9,13},{10,... | collective-permute-start | bytes 2359304 | tf_op jit(solution)/shard_map/ppermute | solution.py:45
  47.7 34.6 %copy-start.5 = (f32[1536]{0:T(1024)S(1)}, f32[1536]{0:T(1024)}, u32[]{:S(2)}) copy-start(f32[1536]{0:T(1024)} %param.13) | copy-start | bytes 18436
  47.7 34.6 %copy-start.6 = (f32[1536]{0:T(1024)S(1)}, f32[1536]{0:T(1024)}, u32[]{:S(2)}) copy-start(f32[1536]{0:T(1024)} %param.12) | copy-start | bytes 18436
  82.3 3.4 %copy-start.3 = (bf16[1536,3,384]{2,0,1:T(8,128)(2,1)S(1)}, bf16[1536,3,384]{2,0,1:T(8,128)(2,1)}, u32[]{:S(2)}) copy-start(bf16[1536,3,384]{2,0,1:T(8,128)(2,1)} %all-gather.3.cloned.1.call-done) | copy-start | bytes 10616836
  85.6 1.1 copy-start.12
  86.6 26.3 %copy-start.2 = (bf16[1,512,1536]{2,1,0:T(8,128)(2,1)S(1)}, bf16[1,512,1536]{2,1,0:T(8,128)(2,1)}, u32[]{:S(2)}) copy-start(bf16[1,512,1536]{2,1,0:T(8,128)(2,1)} %param.11) | copy-start | bytes 4718596
  89.6 25.9 %copy-start.7 = (f32[512]{0:T(512)S(1)}, f32[512]{0:T(512)}, u32[]{:S(2)}) copy-start(f32[512]{0:T(512)} %convert_element_type.70) | copy-start | bytes 6148
  89.6 25.9 %copy-start.10 = (bf16[1,512,512]{2,1,0:T(8,128)(2,1)S(1)}, bf16[1,512,512]{2,1,0:T(8,128)(2,1)}, u32[]{:S(2)}) copy-start(bf16[1,512,512]{2,1,0:T(8,128)(2,1)} %param.19) | copy-start | bytes 1572868
  120.8 127.2 %all-reduce.3.cloned.1.call-start = ((), (), s32[]{:S(2)}) async-start(), calls=%async_computation.4 | async-start | bytes 3932160 | tf_op jit(solution)/shard_map/psum | solution.py:124
  162.2 3.7 %copy-start.9 = (bf16[384,1536]{1,0:T(8,128)(2,1)S(1)}, bf16[384,1536]{1,0:T(8,128)(2,1)}, u32[]{:S(2)}) copy-start(bf16[384,1536]{1,0:T(8,128)(2,1)} %all-gather.5.cloned.1.call-done) | copy-start | bytes 3538948
  166.0 6.1 %copy-start.4 = (bf16[1536,3,384]{2,0,1:T(8,128)(2,1)S(1)}, bf16[1536,3,384]{2,0,1:T(8,128)(2,1)}, u32[]{:S(2)}) copy-start(bf16[1536,3,384]{2,0,1:T(8,128)(2,1)} %all-gather.3.cloned.1.call-done) | copy-start | bytes 10616836
  169.0 4.1 %collective-permute-start.6 = (bf16[32,384]{1,0:T(8,128)(2,1)S(1)}, bf16[32,384]{1,0:T(8,128)(2,1)S(1)}, u32[]{:S(2)}, u32[]{:S(2)}) collective-permute-start(bf16[32,384]{1,0:T(8,128)(2,1)S(1)} %get-tuple-element.5), channel_id=1, source_target_pairs={{0,1},{1,2},{2,3},{3,4},{4,5},{5,6},{6,7},{8,9},{9,10},{10,11},{11... | collective-permute-start | bytes 73736 | tf_op jit(solution)/shard_map/ppermute | solution.py:16
  170.7 4.3 %collective-permute-start.5 = (bf16[32,384]{1,0:T(8,128)(2,1)S(1)}, bf16[32,384]{1,0:T(8,128)(2,1)S(1)}, u32[]{:S(2)}, u32[]{:S(2)}) collective-permute-start(bf16[32,384]{1,0:T(8,128)(2,1)S(1)} %get-tuple-element.4), channel_id=1, source_target_pairs={{1,0},{2,1},{3,2},{4,3},{5,4},{6,5},{7,6},{9,8},{10,9},{11,10},{12... | collective-permute-start | bytes 73736 | tf_op jit(solution)/shard_map/ppermute | solution.py:17
  173.1 2.0 copy-start.14
  174.1 73.9 %copy-start = (bf16[640,1536]{1,0:T(8,128)(2,1)S(1)}, bf16[640,1536]{1,0:T(8,128)(2,1)}, u32[]{:S(2)}) copy-start(bf16[640,1536]{1,0:T(8,128)(2,1)} %param.18) | copy-start | bytes 5898244
  (2 other events, 1.6 us)
Sparse Core Ops, SparseCore 0:
  9.6 72.6 all-gather.2
  83.8 29.0 all-gather.4
  120.9 37.5 reduce-scatter.1
  166.1 81.9 all-reduce.2
